TPU v7x, 256 devices: a whole 4x4x8 slice. The times are simulated.
256 devices in a mesh: hist: 32 (over z, y), second: 8 (over x, core).
Axes of the slice: x: 4, y: 4, z: 8, core: 2. Of those that a mesh axis runs over, the one named last changes fastest.
Arguments:
- history: bfloat16 [128, 64, 128, 2, 128], P('hist', None, 'second'), may hold values from -0.29882812 to 0.29882812
- row_now: float32 [64, 128, 256], P('hist', 'second'), may hold values from -4.2 to 4.2
- coupling: float32 [64, 64], P('hist'), may hold values from 0.5 to 1.5
- step_inverse: float32 [3, 2, 64, 64], replicated, may hold values from -0.5 to 0.5
- start_step: int32 [1], replicated, may hold values from 64 to 124
- history_time: int32 [128], P('hist'), may hold values from 0 to 127, each once
Outputs:
- green_next: float32 [64, 128, 256], P('hist', 'second')
Inputs may be any that keep to these rules, and one draw needn't show every extreme that they name: history_time holds every time from 0 to 127 once.
All inputs are finite; a program needn't handle non-finite values.
Results may differ from a plain program's by a relative error of at most 0.011.
Values may be sent and summed in bfloat16 or wider, within the bound.
A program may use at most 64 MiB of HBM per device.

v0:
```python
import jax
import jax.numpy as jnp
from jax import lax
from jax.sharding import PartitionSpec as P

step_width = 0.05
highest = lax.Precision.HIGHEST


def cubic_term(first_real, first_imag, other_real, other_imag):
    square_real = first_real * first_real - first_imag * first_imag
    square_imag = 2.0 * first_real * first_imag
    return (
        square_real * other_real + square_imag * other_imag,
        square_imag * other_real - square_real * other_imag,
    )


def self_energy(green_row, coupling):
    weight_sq = (coupling * coupling)[:, None, :]
    lesser_real, lesser_imag = (green_row[:, :, 0, 0], green_row[:, :, 0, 1])
    greater_real, greater_imag = (green_row[:, :, 1, 0], green_row[:, :, 1, 1])
    less_real, less_imag = cubic_term(lesser_real, lesser_imag, greater_real, greater_imag)
    more_real, more_imag = cubic_term(greater_real, greater_imag, lesser_real, lesser_imag)
    diff_real = weight_sq * (more_real - less_real)
    diff_imag = weight_sq * (more_imag - less_imag)
    stacked = jnp.stack([diff_real, diff_imag], axis=2)
    return stacked.reshape(green_row.shape[0], green_row.shape[1], 2 * green_row.shape[4]).astype(
        jnp.bfloat16
    )


def advance(green_row, summed, inverse_pair):
    real_sum = summed[:, :, :, 0, 0, :] - summed[:, :, :, 1, 1, :]
    imag_sum = summed[:, :, :, 1, 0, :] + summed[:, :, :, 0, 1, :]
    moved_real = green_row[:, :, :, 0, :] + step_width * real_sum
    moved_imag = green_row[:, :, :, 1, :] + step_width * imag_sum
    inverse_real = inverse_pair[0]
    inverse_imag = inverse_pair[1]
    new_real = jnp.einsum(
        "xa,btma->btmx", inverse_real, moved_real, precision=highest
    ) - jnp.einsum("xa,btma->btmx", inverse_imag, moved_imag, precision=highest)
    new_imag = jnp.einsum(
        "xa,btma->btmx", inverse_real, moved_imag, precision=highest
    ) + jnp.einsum("xa,btma->btmx", inverse_imag, moved_real, precision=highest)
    return jnp.stack([new_real, new_imag], axis=3)


def contract(selected, history_block):
    return jnp.einsum(
        "jsqa,sjtmbp->btmpqa", selected, history_block, preferred_element_type=jnp.float32
    )


def body(history, row_now, coupling, step_inverse, start_step, history_time):
    orbitals = history.shape[1]
    own_rows = row_now.shape[0]
    slab = row_now.shape[1]
    anchor = start_step[0]
    slots = history.shape[0]
    alive_slot = history_time <= anchor
    green_row = row_now.reshape(own_rows, slab, 2, 2, orbitals)
    earlier = []
    for window_step in range(step_inverse.shape[0]):
        energy = self_energy(green_row, coupling)
        by_orbital = lax.all_gather(energy, "hist", axis=0, tiled=True)
        whole_row = lax.all_gather(by_orbital, "second", axis=1, tiled=True)
        energy_left = whole_row.reshape(orbitals, whole_row.shape[1], 2, orbitals)
        selected = jnp.take(energy_left, history_time, axis=1)
        selected = jnp.where(alive_slot[None, :, None, None], selected, jnp.zeros((), jnp.bfloat16))
        history_block = history
        history_block = history_block.reshape(
            slots, orbitals, slab, 2, own_rows * lax.axis_size("hist"), 2
        )
        summed = lax.psum_scatter(
            contract(selected, history_block), "hist", scatter_dimension=0, tiled=True
        )
        for past_index, past_row in enumerate(earlier):
            column = lax.dynamic_index_in_dim(
                energy_left, anchor + 1 + past_index, 1, keepdims=False
            ).astype(jnp.float32)
            summed = summed + jnp.einsum("jqa,btmpj->btmpqa", column, past_row, precision=highest)
        green_row = advance(green_row, summed, step_inverse[window_step])
        earlier.append(green_row)
    return green_row.reshape(own_rows, slab, 4 * orbitals)


def solution(mesh):
    placed = (
        P("hist", None, "second", None, None),
        P("hist", "second", None),
        P("hist", None),
        P(),
        P(),
        P("hist"),
    )
    return jax.shard_map(
        body, mesh=mesh, in_specs=placed, out_specs=P("hist", "second", None), check_vma=False
    )
```

profile of v0, /device:TPU:1, one launch (start us, length us, event | category | flops | bytes accessed | tf_op | source)
XLA Modules:
  0.0 986.8 jit_solution(12834149385297724777)
XLA Ops:
  6.5 0.8 mul.713
  7.3 0.9 reshape.729
  8.4 41.1 %all_gather.18 = bf16[64,16,128]{2,1,0:T(8,128)(2,1)S(1)} all-gather(bf16[2,16,128]{2,1,0:T(8,128)(2,1)S(1)} %convert_element_type.15), channel_id=1, replica_groups=mesh['hist'=32,'second'=8] {'hist'}, dimensions={0}, use_global_device_ids=true | all-gather | bytes 270336 | tf_op jit(solution)/shard_map/all_gather | solution.py:66
  49.5 0.8 copy.305
  51.0 7.6 copy.308
  58.5 7.8 copy.310
  66.3 22.0 %all-gather.4.cloned.1.call-done = bf16[64,128,128]{2,0,1:T(8,128)(2,1)} async-done(((bf16[64,16,128]{2,0,1:T(8,128)(2,1)}), bf16[64,128,128]{2,0,1:T(8,128)(2,1)}) %all-gather.4.cloned.1.call-update) | async-done | bytes 2097168 | tf_op jit(solution)/shard_map/all_gather | solution.py:67
  88.4 3.3 copy.306
  91.7 6.5 copy.307
  98.1 2.8 gather_fusion
  100.9 5.0 fusion.6
  105.9 6.4 copy.311
  112.4 216.2 %reduce-scatter.4.cloned.1.call-done = f32[2,16,2,2,2,64]{5,1,4,3,2,0:T(8,128)} async-done(((f32[64,16,2,2,2,64]{5,1,4,3,2,0:T(8,128)}), f32[2,16,2,2,2,64]{5,1,4,3,2,0:T(8,128)}) %reduce-scatter.4.cloned.1.call-update) | async-done | bytes 65552 | tf_op jit(solution)/shard_map/reduce_scatter | solution.py:75
  328.6 0.8 fusion.41
  330.3 36.3 %all_gather.20 = bf16[64,16,128]{2,1,0:T(8,128)(2,1)S(1)} all-gather(bf16[2,16,128]{2,1,0:T(8,128)(2,1)S(1)} %convert_element_type.16), channel_id=1, replica_groups=mesh['hist'=32,'second'=8] {'hist'}, dimensions={0}, use_global_device_ids=true | all-gather | bytes 270336 | tf_op jit(solution)/shard_map/all_gather | solution.py:66
  366.6 0.8 copy.322
  367.5 43.1 %all-gather.6.cloned.1.call-done = bf16[64,128,128]{2,0,1:T(8,128)(2,1)} async-done(((bf16[64,16,128]{2,0,1:T(8,128)(2,1)}), bf16[64,128,128]{2,0,1:T(8,128)(2,1)}) %all-gather.6.cloned.1.call-update) | async-done | bytes 2097168 | tf_op jit(solution)/shard_map/all_gather | solution.py:67
  410.6 3.3 copy.323
  413.9 6.5 copy.324
  420.4 2.8 gather_fusion.1
  423.1 6.8 fusion.9
  430.0 6.3 copy.327
  436.3 0.2 all-gather.8.cloned.1.call-start
  436.6 2.1 constant_dynamic-slice_fusion.2
  438.7 2.1 copy.329
  440.8 211.6 %reduce-scatter.6.cloned.1.call-done = f32[2,16,2,2,2,64]{5,1,4,3,2,0:T(8,128)} async-done(((f32[64,16,2,2,2,64]{5,1,4,3,2,0:T(8,128)}), f32[2,16,2,2,2,64]{5,1,4,3,2,0:T(8,128)}) %reduce-scatter.6.cloned.1.call-update) | async-done | bytes 65552 | tf_op jit(solution)/shard_map/reduce_scatter | solution.py:75
  652.4 1.1 convolution_add_fusion.2
  653.5 0.2 fusion.45
  653.9 0.2 convolution_add_fusion.4
  654.1 0.2 convolution_subtract_fusion.1
  654.4 36.3 %all_gather.22 = bf16[64,16,128]{2,1,0:T(8,128)(2,1)S(1)} all-gather(bf16[2,16,128]{2,1,0:T(8,128)(2,1)S(1)} %convert_element_type.17), channel_id=1, replica_groups=mesh['hist'=32,'second'=8] {'hist'}, dimensions={0}, use_global_device_ids=true | all-gather | bytes 270336 | tf_op jit(solution)/shard_map/all_gather | solution.py:66
  690.7 0.8 copy.340
  691.5 43.2 %all-gather.8.cloned.1.call-done = bf16[64,128,128]{2,0,1:T(8,128)(2,1)} async-done(((bf16[64,16,128]{2,0,1:T(8,128)(2,1)}), bf16[64,128,128]{2,0,1:T(8,128)(2,1)}) %all-gather.8.cloned.1.call-update) | async-done | bytes 2097168 | tf_op jit(solution)/shard_map/all_gather | solution.py:67
  734.7 3.3 copy.341
  738.1 6.5 copy.342
  744.5 2.8 gather_fusion.2
  747.3 7.0 fusion.12
  754.3 6.3 copy.345
  760.6 3.6 constant_dynamic-slice_fusion
  764.3 2.1 copy.351
  766.4 2.1 copy.346
  768.5 208.5 %reduce-scatter.8.cloned.1.call-done = f32[2,16,2,2,2,64]{5,1,4,3,2,0:T(8,128)} async-done(((f32[64,16,2,2,2,64]{5,1,4,3,2,0:T(8,128)}), f32[2,16,2,2,2,64]{5,1,4,3,2,0:T(8,128)}) %reduce-scatter.8.cloned.1.call-update) | async-done | bytes 65552 | tf_op jit(solution)/shard_map/reduce_scatter | solution.py:75
  977.0 1.1 convolution_add_fusion.1
  978.1 0.2 convolution_add_fusion
  978.3 0.2 fusion.53
  978.7 0.2 fusion.15
  978.9 0.2 fusion.16
  979.2 0.7 reshape.734
  (42 shorter events, 2.0 us)
Async XLA Ops:
  6.5 81.8 %all-gather.4.cloned.1.call-start = ((), (), s32[]{:S(2)}) async-start(), calls=%async_computation.3 | async-start | bytes 2359296 | tf_op jit(solution)/shard_map/all_gather | solution.py:67
  50.3 278.3 %reduce-scatter.4.cloned.1.call-start = ((), (), s32[]{:S(2)}) async-start(), calls=%async_computation.4 | async-start | bytes 4325376 | tf_op jit(solution)/shard_map/reduce_scatter | solution.py:75
  58.5 7.8 copy-start.1
  112.3 217.1 %copy-start = (f32[3,2,64,64]{3,2,1,0:T(8,128)S(1)}, f32[3,2,64,64]{3,2,1,0:T(8,128)}, u32[]{:S(2)}) copy-start(f32[3,2,64,64]{3,2,1,0:T(8,128)} %param.11) | copy-start | bytes 294916
  112.3 298.3 %all-gather.6.cloned.1.call-start = ((), (), s32[]{:S(2)}) async-start(), calls=%async_computation.5 | async-start | bytes 2359296 | tf_op jit(solution)/shard_map/all_gather | solution.py:67
  367.4 285.0 %reduce-scatter.6.cloned.1.call-start = ((), (), s32[]{:S(2)}) async-start(), calls=%async_computation.6 | async-start | bytes 4325376 | tf_op jit(solution)/shard_map/reduce_scatter | solution.py:75
  436.3 298.4 %all-gather.8.cloned.1.call-start = ((), (), s32[]{:S(2)}) async-start(), calls=%async_computation.7 | async-start | bytes 2359296 | tf_op jit(solution)/shard_map/all_gather | solution.py:67
  691.5 285.5 %reduce-scatter.8.cloned.1.call-start = ((), (), s32[]{:S(2)}) async-start(), calls=%async_computation.8 | async-start | bytes 4325376 | tf_op jit(solution)/shard_map/reduce_scatter | solution.py:75
Sparse Core Ops, SparseCore 0:
  50.4 37.9 all-gather.3
  112.4 216.1 reduce-scatter.3
  367.5 43.0 all-gather.5
  436.4 215.8 reduce-scatter.5
  691.6 43.0 all-gather.7
  760.7 216.2 reduce-scatter.7
where the time goes:
time: 993 us; the launch traced here: 987 us
  waiting for transfers between devices  745 us (75%)
  blocking collectives  114 us (11%)
  local copies, waits for them, and re-layouts  88.4 us (9%)
  matrix products  23.5 us (2%)
  between operations  14.5 us (1%)
    reduce_scatter x3, waiting for transfers between devices, body(): lax.psum_scatter(contract(selected, history_block), 'hist', scatter_dimen...  636 us
    all_gather x3, blocking collectives, body(): by_orbital = lax.all_gather(energy, 'hist', axis=0, tiled=True)  114 us
    all_gather x3, waiting for transfers between devices, body(): whole_row = lax.all_gather(by_orbital, 'second', axis=1, tiled=True)  108 us
  transfers between devices with their start and end apart: 6, of which 6 were waited for; matrix products, arithmetic and copies ran while one was open for 3% of the time, Pallas kernels for 0%

commit v1 on v0

v1 whole, which is shorter than its diff:
```python
import functools

import jax
import jax.numpy as jnp
from jax import lax
from jax.experimental import pallas as pl
from jax.experimental.pallas import tpu as pltpu
from jax.sharding import PartitionSpec as P

MESH = pl.DeviceIdType.MESH
HIGHEST = lax.Precision.HIGHEST
STEP_WIDTH = 0.05
CHIPS_Y = 4
F32 = jnp.float32
BF16 = jnp.bfloat16


def cubic_term(first_real, first_imag, other_real, other_imag):
    square_real = first_real * first_real - first_imag * first_imag
    square_imag = 2.0 * first_real * first_imag
    return (
        square_real * other_real + square_imag * other_imag,
        square_imag * other_real - square_real * other_imag,
    )


def turned(pair, half):
    return jnp.concatenate([-pair[:, half:], pair[:, :half]], axis=1)


def wait_bytes(ref, sem):
    pltpu.make_async_copy(ref, ref, sem).wait()


def kernel(
    dims,
    hist_ref,
    row_ref,
    coup_ref,
    inv_ref,
    start_ref,
    time_ref,
    out_ref,
    h2,
    ebuf,
    vbuf,
    onehot,
    sendb,
    recvb,
    sendy,
    recvy,
    zown,
    sendz,
    recvz,
    hist_sem,
    v_send,
    v_recv,
    a_send,
    a_recv,
    b_send,
    b_recv,
    y_send,
    y_recv,
    z_send,
    z_recv,
):
    n_hist, n_second, n_y, order, cuts, steps = dims
    n_z = n_hist // n_y
    own, slab, width = row_ref.shape
    half = width // 4
    pair = 2 * half
    slots = time_ref.shape[0]
    times = ebuf.shape[1]
    rows = own * 2 * slab
    h = lax.axis_index("hist")
    sec = lax.axis_index("second")
    z = h // n_y
    y = lax.rem(h, n_y)

    def hist_peer(d):
        return lax.rem(h + d, n_hist)

    def second_peer(d):
        return lax.rem(sec + d, n_second)

    barrier = pltpu.get_barrier_semaphore()

    @pl.loop(1, n_second)
    def _(d):
        pl.semaphore_signal(barrier, 1, device_id=(h, second_peer(d)), device_id_type=MESH)

    @pl.loop(1, n_hist)
    def _(d):
        pl.semaphore_signal(barrier, 1, device_id=(hist_peer(d), sec), device_id_type=MESH)

    load_hist = pltpu.make_async_copy(hist_ref, h2, hist_sem)
    load_hist.start()

    anchor = start_ref[0].astype(F32)
    row8 = lax.broadcasted_iota(jnp.int32, (8, times), 0)
    tile = jnp.full((8, times), -1.0, F32)
    for s in range(slots):
        held = time_ref[s].astype(F32)
        tile = jnp.where(lax.rem(row8, slots) == s, held, tile)
    vbuf[h] = tile

    weight_sq = coup_ref[...] * coup_ref[...]

    def put_energy(w, green):
        for b in range(own):
            less, more = green[b][0], green[b][1]
            lr, li, mr, mi = less[:, :half], less[:, half:], more[:, :half], more[:, half:]
            less_r, less_i = cubic_term(lr, li, mr, mi)
            more_r, more_i = cubic_term(mr, mi, lr, li)
            weight = weight_sq[b : b + 1, :]
            both = jnp.concatenate([weight * (more_r - less_r), weight * (more_i - less_i)], axis=1)
            ebuf[w, pl.ds(pl.multiple_of(sec * slab, slab), slab), b * pair : (b + 1) * pair] = both.astype(BF16)

    def send_energy(w):
        mine = ebuf.at[w, pl.ds(pl.multiple_of(sec * slab, slab), slab)]

        @pl.loop(1, n_second)
        def _(d):
            pltpu.make_async_remote_copy(
                mine, mine, a_send.at[w], a_recv.at[w], device_id=(h, second_peer(d)), device_id_type=MESH
            ).start()

    green = [[row_ref[b, :, m * pair : (m + 1) * pair] for m in range(2)] for b in range(own)]
    put_energy(0, green)

    pl.semaphore_wait(barrier, n_second - 1 + n_hist - 1)
    send_energy(0)

    @pl.loop(1, n_hist)
    def _(d):
        pltpu.make_async_remote_copy(
            vbuf.at[h], vbuf.at[h], v_send, v_recv, device_id=(hist_peer(d), sec), device_id_type=MESH
        ).start()

    wait_bytes(vbuf.at[0 : n_hist - 1], v_recv)
    asked = vbuf[...].reshape(n_hist * 8, times)
    lane = lax.broadcasted_iota(jnp.int32, (n_hist * 8, times), 1).astype(F32)
    onehot[0 : n_hist * 8, :] = jnp.where((asked == lane) & (asked <= anchor), 1.0, 0.0).astype(BF16)
    row16 = lax.broadcasted_iota(jnp.int32, (16, times), 0)
    lane16 = lax.broadcasted_iota(jnp.int32, (16, times), 1).astype(F32)
    later = anchor + 1.0 + lax.rem(row16, 2).astype(F32)
    onehot[n_hist * 8 : n_hist * 8 + 16, :] = jnp.where((later == lane16) & (row16 < 2 * own), 1.0, 0.0).astype(BF16)

    past = []
    for w in range(steps):
        wait_bytes(ebuf.at[w, 0 : times - slab], a_recv.at[w])
        picked = jnp.dot(onehot[...], ebuf[w], preferred_element_type=F32)
        sub = lax.rem(lax.broadcasted_iota(jnp.int32, (n_hist * 8, pair), 0), 8)
        chosen = jnp.where(sub < slots, picked[: n_hist * 8, :pair], picked[: n_hist * 8, pair:])
        sub8 = lax.broadcasted_iota(jnp.int32, (8, pair), 0)
        extra = picked[n_hist * 8 : n_hist * 8 + 8]
        extra = jnp.where(sub8 < 2, extra[:, :pair], extra[:, pair:])
        piece = jnp.concatenate(
            [chosen.reshape(n_hist, 8, pair), jnp.broadcast_to(extra[None], (n_hist, 8, pair))], axis=1
        )
        sendb[w] = piece.astype(BF16)

        @pl.loop(1, n_hist)
        def _(d, w=w):
            to = hist_peer(d)
            pltpu.make_async_remote_copy(
                sendb.at[w, to], recvb.at[w, h], b_send.at[w], b_recv.at[w], device_id=(to, sec), device_id_type=MESH
            ).start()

        recvb[w, h] = sendb[w, h]
        wait_bytes(recvb.at[w, 0 : n_hist - 1], b_recv.at[w])
        got = recvb[w].astype(F32)
        left = got[:, :8].reshape(n_hist * 8, pair)
        weights = jnp.concatenate([left, turned(left, half)], axis=0).astype(BF16)
        if w == 0:
            load_hist.wait()

        def product(off, first, last):
            to_y = lax.rem(y + off, n_y)
            block = jnp.concatenate([h2[lax.rem(z + order[n], n_z), to_y] for n in range(first, last)], axis=0)
            return jnp.dot(block, weights, preferred_element_type=F32).reshape(last - first, rows, pair)

        for c, (first, last) in enumerate(cuts):
            for off in sorted(range(1, n_y), key=lambda o: -min(o, n_y - o)):
                sendy[w, off - 1, first:last] = product(off, first, last).astype(BF16)
                part = (w, off - 1, pl.ds(first, last - first))
                pltpu.make_async_remote_copy(
                    sendy.at[part],
                    recvy.at[part],
                    y_send.at[w],
                    y_recv.at[w, c],
                    device_id=(z * n_y + lax.rem(y + off, n_y), sec),
                    device_id_type=MESH,
                ).start()
        for first, last in cuts:
            zown[first:last] = product(0, first, last)

        local = [[green[b][m] for m in range(2)] for b in range(own)]
        recent = None
        if w:
            tail = got[:, 8:].reshape(n_hist * 8, pair).astype(BF16)
            rec = [None] * w
            for i in range(w):
                orbital = lax.broadcasted_iota(jnp.int32, (half, n_hist * 8), 0)
                at = lax.broadcasted_iota(jnp.int32, (half, n_hist * 8), 1)
                pick = jnp.where(at == (orbital // own) * 8 + lax.rem(orbital, own) * 2 + i, 1.0, 0.0).astype(BF16)
                column = jnp.dot(pick, tail, preferred_element_type=F32)
                matrix = jnp.concatenate([column, turned(column, half)], axis=0)
                rec[i] = jnp.dot(past[i], matrix, precision=HIGHEST, preferred_element_type=F32)
            recent = rec[0] if w == 1 else rec[0] + rec[1]

        total = None
        for c, (first, last) in enumerate(cuts):
            wait_bytes(recvy.at[w, :, first:last], y_recv.at[w, c])
            for n in range(first, last):
                acc = zown[n]
                for k in range(n_y - 1):
                    acc = acc + recvy[w, k, n].astype(F32)
                if order[n] == 0:
                    total = acc
                    continue
                sendz[w, n] = acc.astype(BF16)
                pltpu.make_async_remote_copy(
                    sendz.at[w, n],
                    recvz.at[w, n],
                    z_send.at[w],
                    z_recv.at[w],
                    device_id=(lax.rem(z + order[n], n_z) * n_y + y, sec),
                    device_id_type=MESH,
                ).start()
        wait_bytes(recvz.at[w], z_recv.at[w])
        for n in range(n_z - 1):
            total = total + recvz[w, n].astype(F32)
        if recent is not None:
            total = total + recent

        current = jnp.concatenate([local[b][m] for b in range(own) for m in range(2)], axis=0)
        moved = current + STEP_WIDTH * total
        real, imag = inv_ref[w, 0], inv_ref[w, 1]
        advance = jnp.concatenate(
            [jnp.concatenate([real, -imag], axis=1), jnp.concatenate([imag, real], axis=1)], axis=0
        )
        new = lax.dot_general(
            moved, advance, (((1,), (1,)), ((), ())), precision=HIGHEST, preferred_element_type=F32
        )
        past.append(new)
        split = new.reshape(own, 2, slab, pair)
        green = [[split[b, m] for m in range(2)] for b in range(own)]
        if w + 1 < steps:
            put_energy(w + 1, green)
            send_energy(w + 1)
        else:
            for b in range(own):
                for m in range(2):
                    out_ref[b, :, m * pair : (m + 1) * pair] = green[b][m]

    wait_bytes(vbuf.at[0 : n_hist - 1], v_send)
    for w in range(steps):
        wait_bytes(ebuf.at[w, 0 : times - slab], a_send.at[w])
        wait_bytes(recvb.at[w, 0 : n_hist - 1], b_send.at[w])
        wait_bytes(recvy.at[w], y_send.at[w])
        wait_bytes(recvz.at[w], z_send.at[w])


def body(n_hist, n_second, n_y, history, row_now, coupling, step_inverse, start_step, history_time):
    slots, orbitals, slab = history.shape[:3]
    own = row_now.shape[0]
    pair = 2 * orbitals
    n_z = n_hist // n_y
    steps = step_inverse.shape[0]
    times = slab * n_second
    rows = own * 2 * slab
    order = sorted(range(n_z), key=lambda d: (-min(d, n_z - d), d))
    cuts = ((0, n_z // 2), (n_z // 2, n_z))
    dims = (n_hist, n_second, n_y, tuple(order), cuts, steps)
    blocks = history.reshape(slots, orbitals, slab, 2, orbitals, 2)
    blocks = blocks.transpose(4, 3, 2, 5, 1, 0).reshape(n_z, n_y, rows, 2 * orbitals * slots)
    vmem = pl.BlockSpec(memory_space=pltpu.VMEM)
    smem = pl.BlockSpec(memory_space=pltpu.SMEM)
    dma = pltpu.SemaphoreType.DMA
    return pl.pallas_call(
        functools.partial(kernel, dims),
        out_shape=jax.ShapeDtypeStruct(row_now.shape, F32),
        in_specs=[pl.BlockSpec(memory_space=pl.ANY), vmem, vmem, vmem, smem, smem],
        out_specs=vmem,
        scratch_shapes=[
            pltpu.VMEM(blocks.shape, BF16),
            pltpu.VMEM((steps, times, own * pair), BF16),
            pltpu.VMEM((n_hist, 8, times), F32),
            pltpu.VMEM((n_hist * 8 + 16, times), BF16),
            pltpu.VMEM((steps, n_hist, 16, pair), BF16),
            pltpu.VMEM((steps, n_hist, 16, pair), BF16),
            pltpu.VMEM((steps, n_y - 1, n_z, rows, pair), BF16),
            pltpu.VMEM((steps, n_y - 1, n_z, rows, pair), BF16),
            pltpu.VMEM((n_z, rows, pair), F32),
            pltpu.VMEM((steps, n_z - 1, rows, pair), BF16),
            pltpu.VMEM((steps, n_z - 1, rows, pair), BF16),
            dma,
            dma,
            dma,
            dma((steps,)),
            dma((steps,)),
            dma((steps,)),
            dma((steps,)),
            dma((steps,)),
            dma((steps, len(cuts))),
            dma((steps,)),
            dma((steps,)),
        ],
        compiler_params=pltpu.CompilerParams(
            collective_id=0, has_side_effects=True, vmem_limit_bytes=32 * 1024 * 1024
        ),
    )(blocks, row_now, coupling, step_inverse, start_step, history_time)


def solution(mesh):
    placed = (
        P("hist", None, "second", None, None),
        P("hist", "second", None),
        P("hist", None),
        P(),
        P(),
        P("hist"),
    )
    return jax.shard_map(
        functools.partial(body, mesh.shape["hist"], mesh.shape["second"], CHIPS_Y),
        mesh=mesh,
        in_specs=placed,
        out_specs=P("hist", "second", None),
        check_vma=False,
    )
```

time: 993 us -> 163 us (0.16)
  waiting for transfers between devices: 745 us -> 0 us
  blocking collectives: 114 us -> 0 us
  Pallas kernels: 0 us -> 83 us
  matrix products: 23.5 us -> 0 us
  between operations: 14.5 us -> 0.7 us
  local copies, waits for them, and re-layouts: 88.4 us -> 76.9 us
    reduce_scatter x3 -> x0, waiting for transfers between devices: 636 us -> none  [body(): lax.psum_scatter(contract(selected, history_block), 'hist', scatter_dimen...]
    all_gather x3 -> x0, blocking collectives: 114 us -> none  [body(): by_orbital = lax.all_gather(energy, 'hist', axis=0, tiled=True)]
    all_gather x3 -> x0, waiting for transfers between devices: 108 us -> none  [body(): whole_row = lax.all_gather(by_orbital, 'second', axis=1, tiled=True)]
    pallas_call x0 -> x1, Pallas kernels: none -> 83 us  [body(): pl.pallas_call(functools.partial(kernel, dims), out_shape=jax.ShapeDtypeS...]
    dot_general x18 -> x0, matrix products: 23.5 us -> none  [the longest x3 18.9 us: contract(): jnp.einsum('jsqa,sjtmbp->btmpqa', selected, history_block, preferred_elem...]
    transpose x3 -> x1, local copies, waits for them, and re-layouts: 19 us -> 31.6 us  [body(): blocks.transpose(4, 3, 2, 5, 1, 0)]
    all_gather x6 -> x0, local copies, waits for them, and re-layouts: 12.2 us -> none  [the longest x3 9.9 us: body(): whole_row = lax.all_gather(by_orbital, 'second', axis=1, tiled=True)]
    dynamic_slice x5 -> x0, local copies, waits for them, and re-layouts: 12.1 us -> none  [body(): lax.dynamic_index_in_dim(energy_left, anchor + 1 + past_index, 1, keepdim...]
  transfers between devices with their start and end apart: 6 -> 0, of which waited for: 6 -> 0; matrix products, arithmetic and copies ran while one was open for 3% -> 0% of each run, Pallas kernels for 0% -> 0%
where the time goes in v1:
time: 163 us; the launch traced here: 161 us
  Pallas kernels  83 us (51%)
  local copies, waits for them, and re-layouts  76.9 us (47%)
    pallas_call x1, Pallas kernels, body(): pl.pallas_call(functools.partial(kernel, dims), out_shape=jax.ShapeDtypeS...  83 us
    reshape x2, local copies, waits for them, and re-layouts, body(): blocks.transpose(4, 3, 2, 5, 1, 0)  37.2 us
    transpose x1, local copies, waits for them, and re-layouts, body(): blocks.transpose(4, 3, 2, 5, 1, 0)  31.6 us
    unnamed x10, local copies, waits for them, and re-layouts  8.14 us

profile of v1, /device:TPU:1, one launch (start us, length us, event | category | flops | bytes accessed | tf_op | source)
XLA Modules:
  0.0 160.7 jit_solution(2904376789374809132)
XLA Ops:
  0.0 7.5 %copy.8 = bf16[4,64,16,2,128]{1,2,4,3,0:T(8,128)(2,1)} copy(bf16[4,64,16,2,128]{4,3,2,1,0:T(2,128)(2,1)} %param.6) | data formatting | bytes 4194304 | tf_op args[0]
  7.5 31.6 %copy.9 = bf16[64,2,16,2,64,4]{2,1,0,5,4,3:T(2,128)(2,1)} copy(bf16[64,2,16,2,64,4]{4,2,3,0,1,5:T(8,128)(2,1)} %bitcast.5) | data formatting | bytes 4194304 | tf_op jit(solution)/shard_map/transpose | solution.py:277
  39.1 31.6 %reshape.7 = bf16[8,4,64,512]{2,1,0,3:T(4,128)(2,1)} reshape(bf16[64,2,16,2,64,4]{2,1,0,5,4,3:T(2,128)(2,1)} %copy.9) | data formatting | bytes 4194304 | tf_op jit(solution)/shard_map/reshape | solution.py:277
  70.7 0.0 copy-start
  70.7 0.0 copy-start.1
  70.7 0.0 copy-start.2
  70.7 0.0 copy-start.3
  70.7 5.6 %copy.10.hist_ref = bf16[8,4,64,512]{3,2,1,0:T(8,128)(2,1)S(1)} copy(bf16[8,4,64,512]{2,1,0,3:T(4,128)(2,1)} %reshape.7) | data formatting | bytes 4194304 | tf_op jit(solution)/shard_map/reshape | solution.py:277
  77.0 0.0 copy-done
  77.0 0.0 copy-done.1
  77.0 0.0 copy-done.2
  77.0 0.0 copy-done.3
  77.0 83.0 %shard_map.64 = f32[2,16,256]{2,1,0:T(8,128)S(1)} custom-call(bf16[8,4,64,512]{3,2,1,0:T(8,128)(2,1)S(1)} %copy.10.hist_ref, f32[2,16,256]{2,1,0:T(8,128)S(1)} %copy-done.1, f32[2,64]{1,0:T(2,128)S(1)} %copy-done.2, f32[3,2,64,64]{3,2,1,0:T(8,128)S(1)} %copy-done, s32[1]{0:T(128)S(6)} %copy.12.start_ref, s32[4]{0:T(128)S(1)} %copy-done.3), custom_call_target="tpu_custom_call" | custom-call | tf_op jit(solution)/shard_map/pallas_call | solution.py:281
  160.1 0.6 copy.13
Async XLA Ops:
  70.7 6.3 %copy-start = (f32[3,2,64,64]{3,2,1,0:T(8,128)S(1)}, f32[3,2,64,64]{3,2,1,0:T(8,128)}, u32[]{:S(2)}) copy-start(f32[3,2,64,64]{3,2,1,0:T(8,128)} %inv_ref.1) | copy-start | bytes 294916
  70.7 6.3 %copy-start.1 = (f32[2,16,256]{2,1,0:T(8,128)S(1)}, f32[2,16,256]{2,1,0:T(8,128)}, u32[]{:S(2)}) copy-start(f32[2,16,256]{2,1,0:T(8,128)} %row_ref.1) | copy-start | bytes 98308
  70.7 6.3 %copy-start.2 = (f32[2,64]{1,0:T(2,128)S(1)}, f32[2,64]{1,0:T(2,128)}, u32[]{:S(2)}) copy-start(f32[2,64]{1,0:T(2,128)} %coup_ref.1) | copy-start | bytes 1540
  70.7 6.3 %copy-start.3 = (s32[4]{0:T(128)S(1)}, s32[4]{0:T(128)}, u32[]{:S(2)}) copy-start(s32[4]{0:T(128)} %time_ref.1) | copy-start | bytes 52

commit v2 on v1

--- a/solution.py
+++ b/solution.py
@@ -41,6 +41,8 @@
     start_ref,
     time_ref,
     out_ref,
+    stored,
+    spread,
     h2,
     ebuf,
     vbuf,
@@ -50,6 +52,7 @@
     sendy,
     recvy,
     zown,
+    summed,
     sendz,
     recvz,
     hist_sem,
@@ -93,7 +96,7 @@
     def _(d):
         pl.semaphore_signal(barrier, 1, device_id=(hist_peer(d), sec), device_id_type=MESH)
 
-    load_hist = pltpu.make_async_copy(hist_ref, h2, hist_sem)
+    load_hist = pltpu.make_async_copy(hist_ref, stored, hist_sem)
     load_hist.start()
 
     anchor = start_ref[0].astype(F32)
@@ -136,6 +139,46 @@
         pltpu.make_async_remote_copy(
             vbuf.at[h], vbuf.at[h], v_send, v_recv, device_id=(hist_peer(d), sec), device_id_type=MESH
         ).start()
+
+    load_hist.wait()
+    wide = 2 * slab
+
+    @pl.loop(0, half)
+    def _(j):
+        for s in range(slots):
+            at = pl.multiple_of((j * slots + s) * wide, wide)
+            spread[pl.ds(at, wide), :] = stored[pl.ds(pl.multiple_of((s * half + j) * wide, wide), wide), :].astype(F32)
+
+    index = lax.broadcasted_iota(jnp.int32, (pair, pair), 0)
+    place = lax.rem(index // own, n_z)
+    depth = jnp.zeros_like(index)
+    for n in range(n_z):
+        depth = jnp.where(place == n, lax.rem(z + order[n], n_z), depth)
+    to_y = lax.rem(lax.rem(index // (own * n_z), n_y) + y, n_y)
+    column = ((depth * n_y + to_y) * own + lax.rem(index, own)) * 2 + index // half
+    turn = jnp.where(lax.broadcasted_iota(jnp.int32, (pair, pair), 1) == column, 1.0, 0.0).astype(BF16)
+    depth_of = half * slots
+    unit = (n_z // len(cuts)) * own
+
+    @pl.loop(0, slab // 2)
+    def _(u):
+        for m in range(2):
+            both = []
+            for k in range(2):
+                block = spread[pl.ds((2 * u + k) * 2 + m, depth_of, stride=wide), :].astype(BF16)
+                both.append(
+                    lax.dot_general(turn, block, (((1,), (1,)), ((), ())), preferred_element_type=F32)
+                )
+            for p in range(2):
+                for off in range(n_y):
+                    for c in range(len(cuts)):
+                        at = p * half + (off * len(cuts) + c) * unit
+                        h2[
+                            off,
+                            c,
+                            pl.ds(pl.multiple_of((m * slab + 2 * u) * unit, 2 * unit), 2 * unit),
+                            p * depth_of : (p + 1) * depth_of,
+                        ] = jnp.concatenate([one[at : at + unit] for one in both], axis=0).astype(BF16)
 
     wait_bytes(vbuf.at[0 : n_hist - 1], v_recv)
     asked = vbuf[...].reshape(n_hist * 8, times)
@@ -172,28 +215,23 @@
         got = recvb[w].astype(F32)
         left = got[:, :8].reshape(n_hist * 8, pair)
         weights = jnp.concatenate([left, turned(left, half)], axis=0).astype(BF16)
-        if w == 0:
-            load_hist.wait()
-
-        def product(off, first, last):
-            to_y = lax.rem(y + off, n_y)
-            block = jnp.concatenate([h2[lax.rem(z + order[n], n_z), to_y] for n in range(first, last)], axis=0)
-            return jnp.dot(block, weights, preferred_element_type=F32).reshape(last - first, rows, pair)
-
-        for c, (first, last) in enumerate(cuts):
+
+        def product(off, c):
+            return jnp.dot(h2[off, c], weights, preferred_element_type=F32)
+
+        for c in range(len(cuts)):
             for off in sorted(range(1, n_y), key=lambda o: -min(o, n_y - o)):
-                sendy[w, off - 1, first:last] = product(off, first, last).astype(BF16)
-                part = (w, off - 1, pl.ds(first, last - first))
+                sendy[w, c, off - 1] = product(off, c).astype(BF16)
                 pltpu.make_async_remote_copy(
-                    sendy.at[part],
-                    recvy.at[part],
+                    sendy.at[w, c, off - 1],
+                    recvy.at[w, c, off - 1],
                     y_send.at[w],
                     y_recv.at[w, c],
                     device_id=(z * n_y + lax.rem(y + off, n_y), sec),
                     device_id_type=MESH,
                 ).start()
-        for first, last in cuts:
-            zown[first:last] = product(0, first, last)
+        for c in range(len(cuts)):
+            zown[c] = product(0, c)
 
         local = [[green[b][m] for m in range(2)] for b in range(own)]
         recent = None
@@ -211,11 +249,15 @@
 
         total = None
         for c, (first, last) in enumerate(cuts):
-            wait_bytes(recvy.at[w, :, first:last], y_recv.at[w, c])
+            wait_bytes(recvy.at[w, c], y_recv.at[w, c])
+            acc = zown[c]
+            for k in range(n_y - 1):
+                acc = acc + recvy[w, c, k].astype(F32)
+            summed[c] = acc
             for n in range(first, last):
-                acc = zown[n]
-                for k in range(n_y - 1):
-                    acc = acc + recvy[w, k, n].astype(F32)
+                acc = jnp.concatenate(
+                    [summed[c, pl.ds((n - first) * own + b, wide, stride=unit), :] for b in range(own)], axis=0
+                )
                 if order[n] == 0:
                     total = acc
                     continue
@@ -273,8 +315,8 @@
     order = sorted(range(n_z), key=lambda d: (-min(d, n_z - d), d))
     cuts = ((0, n_z // 2), (n_z // 2, n_z))
     dims = (n_hist, n_second, n_y, tuple(order), cuts, steps)
-    blocks = history.reshape(slots, orbitals, slab, 2, orbitals, 2)
-    blocks = blocks.transpose(4, 3, 2, 5, 1, 0).reshape(n_z, n_y, rows, 2 * orbitals * slots)
+    part = rows * n_z // len(cuts)
+    blocks = history.reshape(slots * orbitals * slab * 2, pair)
     vmem = pl.BlockSpec(memory_space=pltpu.VMEM)
     smem = pl.BlockSpec(memory_space=pltpu.SMEM)
     dma = pltpu.SemaphoreType.DMA
@@ -285,14 +327,17 @@
         out_specs=vmem,
         scratch_shapes=[
             pltpu.VMEM(blocks.shape, BF16),
+            pltpu.VMEM(blocks.shape, F32),
+            pltpu.VMEM((n_y, len(cuts), part, pair * slots), BF16),
             pltpu.VMEM((steps, times, own * pair), BF16),
             pltpu.VMEM((n_hist, 8, times), F32),
             pltpu.VMEM((n_hist * 8 + 16, times), BF16),
             pltpu.VMEM((steps, n_hist, 16, pair), BF16),
             pltpu.VMEM((steps, n_hist, 16, pair), BF16),
-            pltpu.VMEM((steps, n_y - 1, n_z, rows, pair), BF16),
-            pltpu.VMEM((steps, n_y - 1, n_z, rows, pair), BF16),
-            pltpu.VMEM((n_z, rows, pair), F32),
+            pltpu.VMEM((steps, len(cuts), n_y - 1, part, pair), BF16),
+            pltpu.VMEM((steps, len(cuts), n_y - 1, part, pair), BF16),
+            pltpu.VMEM((len(cuts), part, pair), F32),
+            pltpu.VMEM((len(cuts), part, pair), F32),
             pltpu.VMEM((steps, n_z - 1, rows, pair), BF16),
             pltpu.VMEM((steps, n_z - 1, rows, pair), BF16),
             dma,

time: 163 us -> 89.2 us (0.55); the launches traced: 161 us -> 88.9 us
  local copies, waits for them, and re-layouts: 76.9 us -> 5.22 us
    reshape x2 -> x0, local copies, waits for them, and re-layouts: 37.2 us -> none  [body(): blocks.transpose(4, 3, 2, 5, 1, 0)]
    transpose x1 -> x0, local copies, waits for them, and re-layouts: 31.6 us -> none  [body(): blocks.transpose(4, 3, 2, 5, 1, 0)]
    unnamed x10 -> x11, local copies, waits for them, and re-layouts: 8.14 us -> 5.22 us
where the time goes in v2:
time: 89.2 us; the launch traced here: 88.9 us
  Pallas kernels  83 us (93%)
  local copies, waits for them, and re-layouts  5.22 us (6%)
    pallas_call x1, Pallas kernels, body(): pl.pallas_call(functools.partial(kernel, dims), out_shape=jax.ShapeDtypeS...  83 us
    unnamed x11, local copies, waits for them, and re-layouts  5.22 us

profile of v2, /device:TPU:1, one launch (start us, length us, event | category | flops | bytes accessed | tf_op | source)
XLA Modules:
  0.0 88.9 jit_solution(1023063474089387167)
XLA Ops:
  0.7 0.0 copy-start
  0.7 1.6 %copy-done = bf16[4,64,16,2,128]{4,3,2,1,0:T(2,128)(2,1)S(1)} copy-done((bf16[4,64,16,2,128]{4,3,2,1,0:T(2,128)(2,1)S(1)}, bf16[4,64,16,2,128]{4,3,2,1,0:T(2,128)(2,1)}, u32[]{:S(2)}) %copy-start) | copy-done | bytes 2097176
  2.2 0.0 copy-start.1
  2.2 0.9 %copy-done.1 = f32[3,2,64,64]{3,2,1,0:T(8,128)S(1)} copy-done((f32[3,2,64,64]{3,2,1,0:T(8,128)S(1)}, f32[3,2,64,64]{3,2,1,0:T(8,128)}, u32[]{:S(2)}) %copy-start.1) | copy-done | bytes 98328
  3.2 0.0 copy-start.2
  3.2 0.8 copy-done.2
  3.9 0.0 copy-start.3
  3.9 0.7 copy-done.3
  4.6 0.0 copy-start.4
  4.6 0.7 copy-done.4
  5.3 83.0 %shard_map.64 = f32[2,16,256]{2,1,0:T(8,128)S(1)} custom-call(bf16[8192,128]{1,0:T(8,128)(2,1)S(1)} %bitcast.1, f32[2,16,256]{2,1,0:T(8,128)S(1)} %copy-done.2, f32[2,64]{1,0:T(2,128)S(1)} %copy-done.3, f32[3,2,64,64]{3,2,1,0:T(8,128)S(1)} %copy-done.1, s32[1]{0:T(128)S(6)} %copy.8.start_ref, s32[4]{0:T(128)S(1)} %copy-done.4), custom_call_target="tpu_custom_call" | custom-call | tf_op jit(solution)/shard_map/pallas_call | solution.py:323
  88.3 0.6 copy.9
Async XLA Ops:
  0.7 1.6 %copy-start = (bf16[4,64,16,2,128]{4,3,2,1,0:T(2,128)(2,1)S(1)}, bf16[4,64,16,2,128]{4,3,2,1,0:T(2,128)(2,1)}, u32[]{:S(2)}) copy-start(bf16[4,64,16,2,128]{4,3,2,1,0:T(2,128)(2,1)} %param.6) | copy-start | bytes 6291460
  2.2 0.9 %copy-start.1 = (f32[3,2,64,64]{3,2,1,0:T(8,128)S(1)}, f32[3,2,64,64]{3,2,1,0:T(8,128)}, u32[]{:S(2)}) copy-start(f32[3,2,64,64]{3,2,1,0:T(8,128)} %inv_ref.1) | copy-start | bytes 294916
  3.2 0.8 copy-start.2
  3.9 0.7 copy-start.3
  4.6 0.7 copy-start.4

commit v3 on v2

--- a/solution.py
+++ b/solution.py
@@ -34,13 +34,18 @@
 
 def kernel(
     dims,
-    hist_ref,
+    hist_hbm,
+    row_hbm,
+    coup_hbm,
+    inv_hbm,
+    start_hbm,
+    time_hbm,
+    out_ref,
     row_ref,
     coup_ref,
     inv_ref,
     start_ref,
     time_ref,
-    out_ref,
     stored,
     spread,
     h2,
@@ -55,7 +60,7 @@
     summed,
     sendz,
     recvz,
-    hist_sem,
+    in_sem,
     v_send,
     v_recv,
     a_send,
@@ -80,24 +85,44 @@
     z = h // n_y
     y = lax.rem(h, n_y)
 
-    def hist_peer(d):
-        return lax.rem(h + d, n_hist)
-
-    def second_peer(d):
-        return lax.rem(sec + d, n_second)
+    def outward(k, n):
+        step = (k + 1) // 2
+        return n // 2 + step - 2 * step * lax.rem(k, 2)
+
+    def hist_peer(k):
+        return lax.rem(z + outward(k // n_y, n_z), n_z) * n_y + lax.rem(y + outward(lax.rem(k, n_y), n_y), n_y)
+
+    def second_peer(k):
+        x = lax.rem(sec // 2 + outward(k // 2, n_second // 2), n_second // 2)
+        return x * 2 + lax.rem(lax.rem(sec, 2) + 1 - lax.rem(k, 2), 2)
 
     barrier = pltpu.get_barrier_semaphore()
 
-    @pl.loop(1, n_second)
-    def _(d):
-        pl.semaphore_signal(barrier, 1, device_id=(h, second_peer(d)), device_id_type=MESH)
-
-    @pl.loop(1, n_hist)
-    def _(d):
-        pl.semaphore_signal(barrier, 1, device_id=(hist_peer(d), sec), device_id_type=MESH)
-
-    load_hist = pltpu.make_async_copy(hist_ref, stored, hist_sem)
-    load_hist.start()
+    @pl.loop(0, n_hist - 1)
+    def _(k):
+        pl.semaphore_signal(barrier, 1, device_id=(hist_peer(k), sec), device_id_type=MESH)
+
+    @pl.loop(0, n_second - 1)
+    def _(k):
+        pl.semaphore_signal(barrier, 1, device_id=(h, second_peer(k)), device_id_type=MESH)
+
+    loads = [
+        pltpu.make_async_copy(src, dst, in_sem.at[i])
+        for i, (src, dst) in enumerate(
+            (
+                (start_hbm, start_ref),
+                (time_hbm, time_ref),
+                (coup_hbm, coup_ref),
+                (row_hbm, row_ref),
+                (hist_hbm, stored),
+                (inv_hbm, inv_ref),
+            )
+        )
+    ]
+    for load in loads:
+        load.start()
+    for load in loads[:4]:
+        load.wait()
 
     anchor = start_ref[0].astype(F32)
     row8 = lax.broadcasted_iota(jnp.int32, (8, times), 0)
@@ -122,32 +147,34 @@
     def send_energy(w):
         mine = ebuf.at[w, pl.ds(pl.multiple_of(sec * slab, slab), slab)]
 
-        @pl.loop(1, n_second)
-        def _(d):
+        @pl.loop(0, n_second - 1)
+        def _(k):
             pltpu.make_async_remote_copy(
-                mine, mine, a_send.at[w], a_recv.at[w], device_id=(h, second_peer(d)), device_id_type=MESH
+                mine, mine, a_send.at[w], a_recv.at[w], device_id=(h, second_peer(k)), device_id_type=MESH
             ).start()
 
+    part = 2 * slab * (n_z // len(cuts)) * own
     green = [[row_ref[b, :, m * pair : (m + 1) * pair] for m in range(2)] for b in range(own)]
     put_energy(0, green)
 
-    pl.semaphore_wait(barrier, n_second - 1 + n_hist - 1)
-    send_energy(0)
-
-    @pl.loop(1, n_hist)
-    def _(d):
-        pltpu.make_async_remote_copy(
-            vbuf.at[h], vbuf.at[h], v_send, v_recv, device_id=(hist_peer(d), sec), device_id_type=MESH
-        ).start()
-
-    load_hist.wait()
     wide = 2 * slab
+    loads[4].wait()
 
     @pl.loop(0, half)
     def _(j):
         for s in range(slots):
             at = pl.multiple_of((j * slots + s) * wide, wide)
             spread[pl.ds(at, wide), :] = stored[pl.ds(pl.multiple_of((s * half + j) * wide, wide), wide), :].astype(F32)
+
+    pl.semaphore_wait(barrier, n_second - 1 + n_hist - 1)
+
+    @pl.loop(0, n_hist - 1)
+    def _(k):
+        pltpu.make_async_remote_copy(
+            vbuf.at[h], vbuf.at[h], v_send, v_recv, device_id=(hist_peer(k), sec), device_id_type=MESH
+        ).start()
+
+    send_energy(0)
 
     index = lax.broadcasted_iota(jnp.int32, (pair, pair), 0)
     place = lax.rem(index // own, n_z)
@@ -174,8 +201,8 @@
                     for c in range(len(cuts)):
                         at = p * half + (off * len(cuts) + c) * unit
                         h2[
+                            c,
                             off,
-                            c,
                             pl.ds(pl.multiple_of((m * slab + 2 * u) * unit, 2 * unit), 2 * unit),
                             p * depth_of : (p + 1) * depth_of,
                         ] = jnp.concatenate([one[at : at + unit] for one in both], axis=0).astype(BF16)
@@ -189,6 +216,7 @@
     later = anchor + 1.0 + lax.rem(row16, 2).astype(F32)
     onehot[n_hist * 8 : n_hist * 8 + 16, :] = jnp.where((later == lane16) & (row16 < 2 * own), 1.0, 0.0).astype(BF16)
 
+    loads[5].wait()
     past = []
     for w in range(steps):
         wait_bytes(ebuf.at[w, 0 : times - slab], a_recv.at[w])
@@ -203,9 +231,9 @@
         )
         sendb[w] = piece.astype(BF16)
 
-        @pl.loop(1, n_hist)
-        def _(d, w=w):
-            to = hist_peer(d)
+        @pl.loop(0, n_hist - 1)
+        def _(k, w=w):
+            to = hist_peer(k)
             pltpu.make_async_remote_copy(
                 sendb.at[w, to], recvb.at[w, h], b_send.at[w], b_recv.at[w], device_id=(to, sec), device_id_type=MESH
             ).start()
@@ -216,22 +244,25 @@
         left = got[:, :8].reshape(n_hist * 8, pair)
         weights = jnp.concatenate([left, turned(left, half)], axis=0).astype(BF16)
 
-        def product(off, c):
-            return jnp.dot(h2[off, c], weights, preferred_element_type=F32)
-
         for c in range(len(cuts)):
-            for off in sorted(range(1, n_y), key=lambda o: -min(o, n_y - o)):
-                sendy[w, c, off - 1] = product(off, c).astype(BF16)
-                pltpu.make_async_remote_copy(
-                    sendy.at[w, c, off - 1],
-                    recvy.at[w, c, off - 1],
-                    y_send.at[w],
-                    y_recv.at[w, c],
-                    device_id=(z * n_y + lax.rem(y + off, n_y), sec),
-                    device_id_type=MESH,
-                ).start()
+            product = jnp.dot(
+                h2[c, 1:].reshape((n_y - 1) * part, pair * slots), weights, preferred_element_type=F32
+            ).astype(BF16)
+            for off in range(1, n_y):
+                sendy[w, c, off - 1] = product[(off - 1) * part : off * part]
+            for m in range(2):
+                for off in sorted(range(1, n_y), key=lambda o: -min(o, n_y - o)):
+                    own_m = (w, c, off - 1, pl.ds(m * part // 2, part // 2))
+                    pltpu.make_async_remote_copy(
+                        sendy.at[own_m],
+                        recvy.at[own_m],
+                        y_send.at[w],
+                        y_recv.at[w, c, m],
+                        device_id=(z * n_y + lax.rem(y + off, n_y), sec),
+                        device_id_type=MESH,
+                    ).start()
         for c in range(len(cuts)):
-            zown[c] = product(0, c)
+            zown[c] = jnp.dot(h2[c, 0], weights, preferred_element_type=F32)
 
         local = [[green[b][m] for m in range(2)] for b in range(own)]
         recent = None
@@ -247,36 +278,43 @@
                 rec[i] = jnp.dot(past[i], matrix, precision=HIGHEST, preferred_element_type=F32)
             recent = rec[0] if w == 1 else rec[0] + rec[1]
 
-        total = None
+        totals = [None, None]
         for c, (first, last) in enumerate(cuts):
-            wait_bytes(recvy.at[w, c], y_recv.at[w, c])
-            acc = zown[c]
-            for k in range(n_y - 1):
-                acc = acc + recvy[w, c, k].astype(F32)
-            summed[c] = acc
-            for n in range(first, last):
-                acc = jnp.concatenate(
-                    [summed[c, pl.ds((n - first) * own + b, wide, stride=unit), :] for b in range(own)], axis=0
-                )
-                if order[n] == 0:
-                    total = acc
-                    continue
-                sendz[w, n] = acc.astype(BF16)
-                pltpu.make_async_remote_copy(
-                    sendz.at[w, n],
-                    recvz.at[w, n],
-                    z_send.at[w],
-                    z_recv.at[w],
-                    device_id=(lax.rem(z + order[n], n_z) * n_y + y, sec),
-                    device_id_type=MESH,
-                ).start()
+            for m in range(2):
+                of_m = pl.ds(m * part // 2, part // 2)
+                wait_bytes(recvy.at[w, c, :, of_m], y_recv.at[w, c, m])
+                acc = zown[c, of_m]
+                for k in range(n_y - 1):
+                    acc = acc + recvy[w, c, k, of_m].astype(F32)
+                summed[c, of_m] = acc
+                for n in range(first, last):
+                    piece = jnp.concatenate(
+                        [
+                            summed[c, pl.ds(m * part // 2 + (n - first) * own + b, slab, stride=unit), :]
+                            for b in range(own)
+                        ],
+                        axis=0,
+                    )
+                    if order[n] == 0:
+                        totals[m] = piece
+                        continue
+                    sendz[w, n, m] = piece.astype(BF16)
+                    pltpu.make_async_remote_copy(
+                        sendz.at[w, n, m],
+                        recvz.at[w, n, m],
+                        z_send.at[w],
+                        z_recv.at[w],
+                        device_id=(lax.rem(z + order[n], n_z) * n_y + y, sec),
+                        device_id_type=MESH,
+                    ).start()
         wait_bytes(recvz.at[w], z_recv.at[w])
         for n in range(n_z - 1):
-            total = total + recvz[w, n].astype(F32)
+            totals = [totals[m] + recvz[w, n, m].astype(F32) for m in range(2)]
+        total = jnp.concatenate(totals, axis=0)
         if recent is not None:
             total = total + recent
 
-        current = jnp.concatenate([local[b][m] for b in range(own) for m in range(2)], axis=0)
+        current = jnp.concatenate([local[b][m] for m in range(2) for b in range(own)], axis=0)
         moved = current + STEP_WIDTH * total
         real, imag = inv_ref[w, 0], inv_ref[w, 1]
         advance = jnp.concatenate(
@@ -286,8 +324,8 @@
             moved, advance, (((1,), (1,)), ((), ())), precision=HIGHEST, preferred_element_type=F32
         )
         past.append(new)
-        split = new.reshape(own, 2, slab, pair)
-        green = [[split[b, m] for m in range(2)] for b in range(own)]
+        split = new.reshape(2, own, slab, pair)
+        green = [[split[m, b] for m in range(2)] for b in range(own)]
         if w + 1 < steps:
             put_energy(w + 1, green)
             send_energy(w + 1)
@@ -318,17 +356,21 @@
     part = rows * n_z // len(cuts)
     blocks = history.reshape(slots * orbitals * slab * 2, pair)
     vmem = pl.BlockSpec(memory_space=pltpu.VMEM)
-    smem = pl.BlockSpec(memory_space=pltpu.SMEM)
     dma = pltpu.SemaphoreType.DMA
     return pl.pallas_call(
         functools.partial(kernel, dims),
         out_shape=jax.ShapeDtypeStruct(row_now.shape, F32),
-        in_specs=[pl.BlockSpec(memory_space=pl.ANY), vmem, vmem, vmem, smem, smem],
+        in_specs=[pl.BlockSpec(memory_space=pltpu.HBM)] * 6,
         out_specs=vmem,
         scratch_shapes=[
+            pltpu.VMEM(row_now.shape, F32),
+            pltpu.VMEM(coupling.shape, F32),
+            pltpu.VMEM(step_inverse.shape, F32),
+            pltpu.SMEM(start_step.shape, jnp.int32),
+            pltpu.SMEM(history_time.shape, jnp.int32),
             pltpu.VMEM(blocks.shape, BF16),
             pltpu.VMEM(blocks.shape, F32),
-            pltpu.VMEM((n_y, len(cuts), part, pair * slots), BF16),
+            pltpu.VMEM((len(cuts), n_y, part, pair * slots), BF16),
             pltpu.VMEM((steps, times, own * pair), BF16),
             pltpu.VMEM((n_hist, 8, times), F32),
             pltpu.VMEM((n_hist * 8 + 16, times), BF16),
@@ -338,17 +380,17 @@
             pltpu.VMEM((steps, len(cuts), n_y - 1, part, pair), BF16),
             pltpu.VMEM((len(cuts), part, pair), F32),
             pltpu.VMEM((len(cuts), part, pair), F32),
-            pltpu.VMEM((steps, n_z - 1, rows, pair), BF16),
-            pltpu.VMEM((steps, n_z - 1, rows, pair), BF16),
+            pltpu.VMEM((steps, n_z - 1, 2, own * slab, pair), BF16),
+            pltpu.VMEM((steps, n_z - 1, 2, own * slab, pair), BF16),
+            dma((6,)),
             dma,
             dma,
-            dma,
-            dma((steps,)),
-            dma((steps,)),
-            dma((steps,)),
-            dma((steps,)),
-            dma((steps,)),
-            dma((steps, len(cuts))),
+            dma((steps,)),
+            dma((steps,)),
+            dma((steps,)),
+            dma((steps,)),
+            dma((steps,)),
+            dma((steps, len(cuts), 2)),
             dma((steps,)),
             dma((steps,)),
         ],

time: 89.2 us -> 83.1 us (0.932)
  Pallas kernels: 83 us -> 77 us
    pallas_call x1, Pallas kernels: 83 us -> 77 us  [body(): pl.pallas_call(functools.partial(kernel, dims), out_shape=jax.ShapeDtypeS...]
where the time goes in v3:
time: 83.1 us; the launch traced here: 82.9 us
  Pallas kernels  77 us (93%)
  local copies, waits for them, and re-layouts  5.22 us (6%)
    pallas_call x1, Pallas kernels, body(): pl.pallas_call(functools.partial(kernel, dims), out_shape=jax.ShapeDtypeS...  77 us
    unnamed x11, local copies, waits for them, and re-layouts  5.22 us

profile of v3, /device:TPU:1, one launch (start us, length us, event | category | flops | bytes accessed | tf_op | source)
XLA Modules:
  0.0 82.9 jit_solution(17295998840273402723)
XLA Ops:
  0.7 0.0 copy-start
  0.7 1.6 %copy-done = bf16[4,64,16,2,128]{4,3,2,1,0:T(2,128)(2,1)S(1)} copy-done((bf16[4,64,16,2,128]{4,3,2,1,0:T(2,128)(2,1)S(1)}, bf16[4,64,16,2,128]{4,3,2,1,0:T(2,128)(2,1)}, u32[]{:S(2)}) %copy-start) | copy-done | bytes 2097176
  2.2 0.0 copy-start.1
  2.2 0.9 %copy-done.1 = f32[3,2,64,64]{3,2,1,0:T(8,128)S(1)} copy-done((f32[3,2,64,64]{3,2,1,0:T(8,128)S(1)}, f32[3,2,64,64]{3,2,1,0:T(8,128)}, u32[]{:S(2)}) %copy-start.1) | copy-done | bytes 98328
  3.2 0.0 copy-start.2
  3.2 0.8 copy-done.2
  3.9 0.0 copy-start.3
  3.9 0.7 copy-done.3
  4.6 0.0 copy-start.4
  4.6 0.7 copy-done.4
  5.3 77.0 %shard_map.64 = f32[2,16,256]{2,1,0:T(8,128)S(1)} custom-call(bf16[8192,128]{1,0:T(8,128)(2,1)S(1)} %bitcast.1, f32[2,16,256]{2,1,0:T(8,128)S(1)} %copy-done.2, f32[2,64]{1,0:T(2,128)S(1)} %copy-done.3, f32[3,2,64,64]{3,2,1,0:T(8,128)S(1)} %copy-done.1, s32[1]{0:T(128)S(6)} %copy.8.start_hbm, s32[4]{0:T(128)S(1)} %copy-done.4), custom_call_target="tpu_custom_call" | custom-call | tf_op jit(solution)/shard_map/pallas_call | solution.py:360
  82.3 0.6 copy.9
Async XLA Ops:
  0.7 1.6 %copy-start = (bf16[4,64,16,2,128]{4,3,2,1,0:T(2,128)(2,1)S(1)}, bf16[4,64,16,2,128]{4,3,2,1,0:T(2,128)(2,1)}, u32[]{:S(2)}) copy-start(bf16[4,64,16,2,128]{4,3,2,1,0:T(2,128)(2,1)} %param.6) | copy-start | bytes 6291460
  2.2 0.9 %copy-start.1 = (f32[3,2,64,64]{3,2,1,0:T(8,128)S(1)}, f32[3,2,64,64]{3,2,1,0:T(8,128)}, u32[]{:S(2)}) copy-start(f32[3,2,64,64]{3,2,1,0:T(8,128)} %inv_hbm.1) | copy-start | bytes 294916
  3.2 0.8 copy-start.2
  3.9 0.7 copy-start.3
  4.6 0.7 copy-start.4

commit v4 on v3

v4 whole, which is shorter than its diff:
```python
import functools

import jax
import jax.numpy as jnp
from jax import lax
from jax.experimental import pallas as pl
from jax.experimental.pallas import tpu as pltpu
from jax.sharding import PartitionSpec as P

MESH = pl.DeviceIdType.MESH
HIGHEST = lax.Precision.HIGHEST
STEP_WIDTH = 0.05
CHIPS_Y = 4
F32 = jnp.float32
BF16 = jnp.bfloat16


def cubic_term(first_real, first_imag, other_real, other_imag):
    square_real = first_real * first_real - first_imag * first_imag
    square_imag = 2.0 * first_real * first_imag
    return (
        square_real * other_real + square_imag * other_imag,
        square_imag * other_real - square_real * other_imag,
    )


def turned(pair, half):
    return jnp.concatenate([-pair[:, half:], pair[:, :half]], axis=1)


def wait_bytes(ref, sem):
    pltpu.make_async_copy(ref, ref, sem).wait()


def kernel(
    dims,
    hist_hbm,
    row_hbm,
    coup_hbm,
    inv_hbm,
    start_hbm,
    time_hbm,
    out_ref,
    row_ref,
    coup_ref,
    inv_ref,
    start_ref,
    time_ref,
    stored,
    spread,
    turned_hist,
    held,
    ebuf,
    vbuf,
    onehot,
    sendb,
    recvb,
    sendx,
    recvx,
    summed,
    sendz,
    recvz,
    in_sem,
    v_send,
    v_recv,
    a_send,
    a_recv,
    b_send,
    b_recv,
    x_send,
    x_recv,
    h_send,
    h_recv,
    z_send,
    z_recv,
):
    n_hist, n_second, n_y, order, steps = dims
    n_z = n_hist // n_y
    own, slab, width = row_ref.shape
    half = width // 4
    pair = 2 * half
    slots = time_ref.shape[0]
    times = ebuf.shape[1]
    rows = own * 2 * slab
    h = lax.axis_index("hist")
    sec = lax.axis_index("second")
    z = h // n_y
    y = lax.rem(h, n_y)

    def outward(k, n):
        step = (k + 1) // 2
        return n // 2 + step - 2 * step * lax.rem(k, 2)

    def hist_peer(k):
        return lax.rem(z + outward(k // n_y, n_z), n_z) * n_y + lax.rem(y + outward(lax.rem(k, n_y), n_y), n_y)

    def second_peer(k):
        x = lax.rem(sec // 2 + outward(k // 2, n_second // 2), n_second // 2)
        return x * 2 + lax.rem(lax.rem(sec, 2) + 1 - lax.rem(k, 2), 2)

    barrier = pltpu.get_barrier_semaphore()

    @pl.loop(0, n_hist - 1)
    def _(k):
        pl.semaphore_signal(barrier, 1, device_id=(hist_peer(k), sec), device_id_type=MESH)

    @pl.loop(0, n_second - 1)
    def _(k):
        pl.semaphore_signal(barrier, 1, device_id=(h, second_peer(k)), device_id_type=MESH)

    loads = [
        pltpu.make_async_copy(src, dst, in_sem.at[i])
        for i, (src, dst) in enumerate(
            (
                (start_hbm, start_ref),
                (time_hbm, time_ref),
                (coup_hbm, coup_ref),
                (row_hbm, row_ref),
                (hist_hbm, stored),
                (inv_hbm, inv_ref),
            )
        )
    ]
    for load in loads:
        load.start()
    for load in loads[:4]:
        load.wait()

    anchor = start_ref[0].astype(F32)
    row8 = lax.broadcasted_iota(jnp.int32, (8, times), 0)
    tile = jnp.full((8, times), -1.0, F32)
    for s in range(slots):
        tile = jnp.where(lax.rem(row8, slots) == s, time_ref[s].astype(F32), tile)
    vbuf[h] = tile

    weight_sq = coup_ref[...] * coup_ref[...]

    def put_energy(w, green):
        for b in range(own):
            less, more = green[b][0], green[b][1]
            lr, li, mr, mi = less[:, :half], less[:, half:], more[:, :half], more[:, half:]
            less_r, less_i = cubic_term(lr, li, mr, mi)
            more_r, more_i = cubic_term(mr, mi, lr, li)
            weight = weight_sq[b : b + 1, :]
            both = jnp.concatenate([weight * (more_r - less_r), weight * (more_i - less_i)], axis=1)
            ebuf[w, pl.ds(pl.multiple_of(sec * slab, slab), slab), b * pair : (b + 1) * pair] = both.astype(BF16)

    def send_energy(w):
        mine = ebuf.at[w, pl.ds(pl.multiple_of(sec * slab, slab), slab)]

        @pl.loop(0, n_second - 1)
        def _(k):
            pltpu.make_async_remote_copy(
                mine, mine, a_send.at[w], a_recv.at[w], device_id=(h, second_peer(k)), device_id_type=MESH
            ).start()

    group = n_z * own
    part = 2 * slab * group
    green = [[row_ref[b, :, m * pair : (m + 1) * pair] for m in range(2)] for b in range(own)]
    put_energy(0, green)

    pl.semaphore_wait(barrier, n_second - 1 + n_hist - 1)

    @pl.loop(0, n_hist - 1)
    def _(k):
        pltpu.make_async_remote_copy(
            vbuf.at[h], vbuf.at[h], v_send, v_recv, device_id=(hist_peer(k), sec), device_id_type=MESH
        ).start()

    send_energy(0)

    wide = 2 * slab
    loads[4].wait()

    @pl.loop(0, half)
    def _(j):
        for s in range(slots):
            at = pl.multiple_of((j * slots + s) * wide, wide)
            spread[pl.ds(at, wide), :] = stored[pl.ds(pl.multiple_of((s * half + j) * wide, wide), wide), :].astype(F32)

    index = lax.broadcasted_iota(jnp.int32, (pair, pair), 0)
    place = lax.rem(index // own, n_z)
    depth = jnp.zeros_like(index)
    for n in range(n_z):
        depth = jnp.where(place == n, lax.rem(z + order[n], n_z), depth)
    to_y = lax.rem(lax.rem(index // (own * n_z), n_y) + y, n_y)
    column = ((depth * n_y + to_y) * own + lax.rem(index, own)) * 2 + index // half
    turn = jnp.where(lax.broadcasted_iota(jnp.int32, (pair, pair), 1) == column, 1.0, 0.0).astype(BF16)
    depth_of = half * slots

    @pl.loop(0, slab)
    def _(t):
        for m in range(2):
            block = spread[pl.ds(t * 2 + m, depth_of, stride=wide), :].astype(BF16)
            columns = lax.dot_general(turn, block, (((1,), (1,)), ((), ())), preferred_element_type=F32).astype(BF16)
            for p in range(2):
                for off in range(n_y):
                    at = p * half + off * group
                    turned_hist[
                        off,
                        pl.ds(pl.multiple_of((m * slab + t) * group, group), group),
                        p * depth_of : (p + 1) * depth_of,
                    ] = columns[at : at + group]

    for off in sorted(range(1, n_y), key=lambda o: -min(o, n_y - o)):
        pltpu.make_async_remote_copy(
            turned_hist.at[off],
            held.at[y],
            h_send,
            h_recv,
            device_id=(z * n_y + lax.rem(y + off, n_y), sec),
            device_id_type=MESH,
        ).start()
    held[y] = turned_hist[0]

    wait_bytes(vbuf.at[0 : n_hist - 1], v_recv)
    asked = vbuf[...].reshape(n_hist * 8, times)
    lane = lax.broadcasted_iota(jnp.int32, (n_hist * 8, times), 1).astype(F32)
    onehot[0 : n_hist * 8, :] = jnp.where((asked == lane) & (asked <= anchor), 1.0, 0.0).astype(BF16)
    row16 = lax.broadcasted_iota(jnp.int32, (16, times), 0)
    lane16 = lax.broadcasted_iota(jnp.int32, (16, times), 1).astype(F32)
    later = anchor + 1.0 + lax.rem(row16, 2).astype(F32)
    onehot[n_hist * 8 : n_hist * 8 + 16, :] = jnp.where((later == lane16) & (row16 < 2 * own), 1.0, 0.0).astype(BF16)

    loads[5].wait()
    past = []
    for w in range(steps):
        wait_bytes(ebuf.at[w, 0 : times - slab], a_recv.at[w])
        picked = jnp.dot(onehot[...], ebuf[w], preferred_element_type=F32)
        sub = lax.rem(lax.broadcasted_iota(jnp.int32, (n_hist * 8, pair), 0), 8)
        chosen = jnp.where(sub < slots, picked[: n_hist * 8, :pair], picked[: n_hist * 8, pair:])
        sendb[w] = chosen.reshape(n_z, n_y * 8, pair).astype(BF16)
        if w:
            extra = picked[n_hist * 8 : n_hist * 8 + 16]
            sub16 = lax.broadcasted_iota(jnp.int32, (16, pair), 0)
            sendx[w] = jnp.where(sub16 < 2, extra[:, :pair], extra[:, pair:]).astype(BF16)

        @pl.loop(0, n_hist - 1)
        def _(k, w=w):
            to = hist_peer(k)
            pltpu.make_async_remote_copy(
                sendb.at[w, to // n_y],
                recvb.at[w, h],
                b_send.at[w],
                b_recv.at[w],
                device_id=(to, sec),
                device_id_type=MESH,
            ).start()

        recvb[w, h] = sendb[w, z]
        if w:

            @pl.loop(0, n_hist - 1)
            def _(k, w=w):
                pltpu.make_async_remote_copy(
                    sendx.at[w],
                    recvx.at[w, h],
                    x_send.at[w],
                    x_recv.at[w],
                    device_id=(hist_peer(k), sec),
                    device_id_type=MESH,
                ).start()

            recvx[w, h] = sendx[w]
        wait_bytes(recvb.at[w, 0 : n_hist - 1], b_recv.at[w])
        got = recvb[w].astype(F32)
        if w == 0:
            wait_bytes(held.at[0 : n_y - 1], h_recv)

        product = None
        for k in range(n_y):
            left = got[:, k * 8 : (k + 1) * 8].reshape(n_hist * 8, pair)
            weights = jnp.concatenate([left, turned(left, half)], axis=0).astype(BF16)
            term = jnp.dot(held[k], weights, preferred_element_type=F32)
            product = term if product is None else product + term
        summed[...] = product
        total = None
        for n in range(n_z):
            piece = jnp.concatenate(
                [summed[pl.ds(n * own + b, 2 * slab, stride=group), :] for b in range(own)], axis=0
            )
            if order[n] == 0:
                total = piece
                continue
            sendz[w, n] = piece.astype(BF16)
            pltpu.make_async_remote_copy(
                sendz.at[w, n],
                recvz.at[w, n],
                z_send.at[w],
                z_recv.at[w],
                device_id=(lax.rem(z + order[n], n_z) * n_y + y, sec),
                device_id_type=MESH,
            ).start()

        local = [[green[b][m] for m in range(2)] for b in range(own)]
        recent = None
        if w:
            wait_bytes(recvx.at[w, 0 : n_hist - 1], x_recv.at[w])
            tail = recvx[w].reshape(n_hist * 16, pair)
            rec = [None] * w
            for i in range(w):
                orbital = lax.broadcasted_iota(jnp.int32, (half, n_hist * 16), 0)
                at = lax.broadcasted_iota(jnp.int32, (half, n_hist * 16), 1)
                pick = jnp.where(at == (orbital // own) * 16 + lax.rem(orbital, own) * 2 + i, 1.0, 0.0).astype(BF16)
                column = jnp.dot(pick, tail, preferred_element_type=F32)
                matrix = jnp.concatenate([column, turned(column, half)], axis=0)
                rec[i] = jnp.dot(past[i], matrix, precision=HIGHEST, preferred_element_type=F32)
            recent = rec[0] if w == 1 else rec[0] + rec[1]

        wait_bytes(recvz.at[w], z_recv.at[w])
        for n in range(n_z - 1):
            total = total + recvz[w, n].astype(F32)
        if recent is not None:
            total = total + recent

        current = jnp.concatenate([local[b][m] for b in range(own) for m in range(2)], axis=0)
        moved = current + STEP_WIDTH * total
        real, imag = inv_ref[w, 0], inv_ref[w, 1]
        advance = jnp.concatenate(
            [jnp.concatenate([real, -imag], axis=1), jnp.concatenate([imag, real], axis=1)], axis=0
        )
        new = lax.dot_general(
            moved, advance, (((1,), (1,)), ((), ())), precision=HIGHEST, preferred_element_type=F32
        )
        past.append(new)
        split = new.reshape(own, 2, slab, pair)
        green = [[split[b, m] for m in range(2)] for b in range(own)]
        if w + 1 < steps:
            put_energy(w + 1, green)
            send_energy(w + 1)
        else:
            for b in range(own):
                for m in range(2):
                    out_ref[b, :, m * pair : (m + 1) * pair] = green[b][m]

    wait_bytes(vbuf.at[0 : n_hist - 1], v_send)
    wait_bytes(held.at[0 : n_y - 1], h_send)
    for w in range(steps):
        wait_bytes(ebuf.at[w, 0 : times - slab], a_send.at[w])
        wait_bytes(recvb.at[w, 0 : n_hist - 1], b_send.at[w])
        if w:
            wait_bytes(recvx.at[w, 0 : n_hist - 1], x_send.at[w])
        wait_bytes(recvz.at[w], z_send.at[w])


def body(n_hist, n_second, n_y, history, row_now, coupling, step_inverse, start_step, history_time):
    slots, orbitals, slab = history.shape[:3]
    own = row_now.shape[0]
    pair = 2 * orbitals
    n_z = n_hist // n_y
    steps = step_inverse.shape[0]
    times = slab * n_second
    rows = own * 2 * slab
    order = sorted(range(n_z), key=lambda d: (-min(d, n_z - d), d))
    dims = (n_hist, n_second, n_y, tuple(order), steps)
    part = rows * n_z
    blocks = history.reshape(slots * orbitals * slab * 2, pair)
    vmem = pl.BlockSpec(memory_space=pltpu.VMEM)
    dma = pltpu.SemaphoreType.DMA
    return pl.pallas_call(
        functools.partial(kernel, dims),
        out_shape=jax.ShapeDtypeStruct(row_now.shape, F32),
        in_specs=[pl.BlockSpec(memory_space=pltpu.HBM)] * 6,
        out_specs=vmem,
        scratch_shapes=[
            pltpu.VMEM(row_now.shape, F32),
            pltpu.VMEM(coupling.shape, F32),
            pltpu.VMEM(step_inverse.shape, F32),
            pltpu.SMEM(start_step.shape, jnp.int32),
            pltpu.SMEM(history_time.shape, jnp.int32),
            pltpu.VMEM(blocks.shape, BF16),
            pltpu.VMEM(blocks.shape, F32),
            pltpu.VMEM((n_y, part, pair * slots), BF16),
            pltpu.VMEM((n_y, part, pair * slots), BF16),
            pltpu.VMEM((steps, times, own * pair), BF16),
            pltpu.VMEM((n_hist, 8, times), F32),
            pltpu.VMEM((n_hist * 8 + 16, times), BF16),
            pltpu.VMEM((steps, n_z, n_y * 8, pair), BF16),
            pltpu.VMEM((steps, n_hist, n_y * 8, pair), BF16),
            pltpu.VMEM((steps, 16, pair), BF16),
            pltpu.VMEM((steps, n_hist, 16, pair), BF16),
            pltpu.VMEM((part, pair), F32),
            pltpu.VMEM((steps, n_z - 1, rows, pair), BF16),
            pltpu.VMEM((steps, n_z - 1, rows, pair), BF16),
            dma((6,)),
            dma,
            dma,
            dma((steps,)),
            dma((steps,)),
            dma((steps,)),
            dma((steps,)),
            dma((steps,)),
            dma((steps,)),
            dma,
            dma,
            dma((steps,)),
            dma((steps,)),
        ],
        compiler_params=pltpu.CompilerParams(
            collective_id=0, has_side_effects=True, vmem_limit_bytes=63 * 1024 * 1024
        ),
    )(blocks, row_now, coupling, step_inverse, start_step, history_time)


def solution(mesh):
    placed = (
        P("hist", None, "second", None, None),
        P("hist", "second", None),
        P("hist", None),
        P(),
        P(),
        P("hist"),
    )
    return jax.shard_map(
        functools.partial(body, mesh.shape["hist"], mesh.shape["second"], CHIPS_Y),
        mesh=mesh,
        in_specs=placed,
        out_specs=P("hist", "second", None),
        check_vma=False,
    )
```

time: 83.1 us -> 93.6 us (1.13)
  Pallas kernels: 77 us -> 91.4 us
  local copies, waits for them, and re-layouts: 5.22 us -> 1.38 us
    pallas_call x1, Pallas kernels: 77 us -> 91.4 us  [body(): pl.pallas_call(functools.partial(kernel, dims), out_shape=jax.ShapeDtypeS...]
    unnamed x11 -> x1, local copies, waits for them, and re-layouts: 5.22 us -> 1.38 us
where the time goes in v4:
time: 93.6 us; the launch traced here: 93.4 us
  Pallas kernels  91.4 us (98%)
  local copies, waits for them, and re-layouts  1.38 us (1%)
    pallas_call x1, Pallas kernels, body(): pl.pallas_call(functools.partial(kernel, dims), out_shape=jax.ShapeDtypeS...  91.4 us

profile of v4, /device:TPU:1, one launch (start us, length us, event | category | flops | bytes accessed | tf_op | source)
XLA Modules:
  0.0 93.4 jit_solution(9732821384086349402)
XLA Ops:
  0.7 91.4 %shard_map.64 = f32[2,16,256]{2,1,0:T(8,128)} custom-call(bf16[8192,128]{1,0:T(8,128)(2,1)} %bitcast.1, f32[2,16,256]{2,1,0:T(8,128)} %row_hbm.1, f32[2,64]{1,0:T(2,128)} %coup_hbm.1, f32[3,2,64,64]{3,2,1,0:T(8,128)} %inv_hbm.1, s32[1]{0:T(128)S(6)} %copy.8.start_hbm, s32[4]{0:T(128)} %time_hbm.1), custom_call_target="tpu_custom_call" | custom-call | tf_op jit(solution)/shard_map/pallas_call | solution.py:360
  92.0 1.4 %copy.9 = f32[2,16,256]{2,1,0:T(8,128)} copy(f32[2,16,256]{2,1,0:T(8,128)} %shard_map.64) | data formatting | bytes 65536

commit v5 on v3

--- a/solution.py
+++ b/solution.py
@@ -395,7 +395,7 @@
             dma((steps,)),
         ],
         compiler_params=pltpu.CompilerParams(
-            collective_id=0, has_side_effects=True, vmem_limit_bytes=32 * 1024 * 1024
+            collective_id=0, has_side_effects=True, vmem_limit_bytes=63 * 1024 * 1024
         ),
     )(blocks, row_now, coupling, step_inverse, start_step, history_time)
 

time: 83.1 us -> 80.1 us (0.964); the launches traced: 82.9 us -> 78.6 us
  local copies, waits for them, and re-layouts: 5.22 us -> 1.38 us
    unnamed x11 -> x1, local copies, waits for them, and re-layouts: 5.22 us -> 1.38 us
where the time goes in v5:
time: 80.1 us; the launch traced here: 78.6 us
  Pallas kernels  76.5 us (96%)
  local copies, waits for them, and re-layouts  1.38 us (2%)
    pallas_call x1, Pallas kernels, body(): pl.pallas_call(functools.partial(kernel, dims), out_shape=jax.ShapeDtypeS...  76.5 us

profile of v5, /device:TPU:1, one launch (start us, length us, event | category | flops | bytes accessed | tf_op | source)
XLA Modules:
  0.0 78.6 jit_solution(4116947690087459906)
XLA Ops:
  0.7 76.5 %shard_map.64 = f32[2,16,256]{2,1,0:T(8,128)} custom-call(bf16[8192,128]{1,0:T(8,128)(2,1)} %bitcast.1, f32[2,16,256]{2,1,0:T(8,128)} %row_hbm.1, f32[2,64]{1,0:T(2,128)} %coup_hbm.1, f32[3,2,64,64]{3,2,1,0:T(8,128)} %inv_hbm.1, s32[1]{0:T(128)S(6)} %copy.8.start_hbm, s32[4]{0:T(128)} %time_hbm.1), custom_call_target="tpu_custom_call" | custom-call | tf_op jit(solution)/shard_map/pallas_call | solution.py:360
  77.2 1.4 %copy.9 = f32[2,16,256]{2,1,0:T(8,128)} copy(f32[2,16,256]{2,1,0:T(8,128)} %shard_map.64) | data formatting | bytes 65536

commit v6 on v5

--- a/solution.py
+++ b/solution.py
@@ -89,18 +89,17 @@
         step = (k + 1) // 2
         return n // 2 + step - 2 * step * lax.rem(k, 2)
 
-    def hist_peer(k):
-        return lax.rem(z + outward(k // n_y, n_z), n_z) * n_y + lax.rem(y + outward(lax.rem(k, n_y), n_y), n_y)
-
     def second_peer(k):
         x = lax.rem(sec // 2 + outward(k // 2, n_second // 2), n_second // 2)
         return x * 2 + lax.rem(lax.rem(sec, 2) + 1 - lax.rem(k, 2), 2)
 
+    far_first = sorted(((dz, dy) for dz in range(n_z) for dy in range(n_y) if dz or dy), key=lambda d: -min(d[0], n_z - d[0]) - min(d[1], n_y - d[1]))
+
     barrier = pltpu.get_barrier_semaphore()
 
-    @pl.loop(0, n_hist - 1)
-    def _(k):
-        pl.semaphore_signal(barrier, 1, device_id=(hist_peer(k), sec), device_id_type=MESH)
+    for dz, dy in far_first:
+        to = lax.rem(z + dz, n_z) * n_y + lax.rem(y + dy, n_y)
+        pl.semaphore_signal(barrier, 1, device_id=(to, sec), device_id_type=MESH)
 
     @pl.loop(0, n_second - 1)
     def _(k):
@@ -168,10 +167,10 @@
 
     pl.semaphore_wait(barrier, n_second - 1 + n_hist - 1)
 
-    @pl.loop(0, n_hist - 1)
-    def _(k):
+    for dz, dy in far_first:
+        to = lax.rem(z + dz, n_z) * n_y + lax.rem(y + dy, n_y)
         pltpu.make_async_remote_copy(
-            vbuf.at[h], vbuf.at[h], v_send, v_recv, device_id=(hist_peer(k), sec), device_id_type=MESH
+            vbuf.at[h], vbuf.at[h], v_send, v_recv, device_id=(to, sec), device_id_type=MESH
         ).start()
 
     send_energy(0)
@@ -231,9 +230,8 @@
         )
         sendb[w] = piece.astype(BF16)
 
-        @pl.loop(0, n_hist - 1)
-        def _(k, w=w):
-            to = hist_peer(k)
+        for dz, dy in far_first:
+            to = lax.rem(z + dz, n_z) * n_y + lax.rem(y + dy, n_y)
             pltpu.make_async_remote_copy(
                 sendb.at[w, to], recvb.at[w, h], b_send.at[w], b_recv.at[w], device_id=(to, sec), device_id_type=MESH
             ).start()
@@ -245,22 +243,23 @@
         weights = jnp.concatenate([left, turned(left, half)], axis=0).astype(BF16)
 
         for c in range(len(cuts)):
-            product = jnp.dot(
-                h2[c, 1:].reshape((n_y - 1) * part, pair * slots), weights, preferred_element_type=F32
-            ).astype(BF16)
-            for off in range(1, n_y):
-                sendy[w, c, off - 1] = product[(off - 1) * part : off * part]
-            for m in range(2):
-                for off in sorted(range(1, n_y), key=lambda o: -min(o, n_y - o)):
-                    own_m = (w, c, off - 1, pl.ds(m * part // 2, part // 2))
-                    pltpu.make_async_remote_copy(
-                        sendy.at[own_m],
-                        recvy.at[own_m],
-                        y_send.at[w],
-                        y_recv.at[w, c, m],
-                        device_id=(z * n_y + lax.rem(y + off, n_y), sec),
-                        device_id_type=MESH,
-                    ).start()
+            def send(off, m, c=c):
+                own_m = (w, c, off - 1, pl.ds(m * part // 2, part // 2))
+                pltpu.make_async_remote_copy(
+                    sendy.at[own_m],
+                    recvy.at[own_m],
+                    y_send.at[w],
+                    y_recv.at[w, c, m],
+                    device_id=(z * n_y + lax.rem(y + off, n_y), sec),
+                    device_id_type=MESH,
+                ).start()
+
+            offs = sorted(range(1, n_y), key=lambda o: -min(o, n_y - o))
+            for off in offs:
+                sendy[w, c, off - 1] = jnp.dot(h2[c, off], weights, preferred_element_type=F32).astype(BF16)
+                send(off, 0)
+            for off in offs:
+                send(off, 1)
         for c in range(len(cuts)):
             zown[c] = jnp.dot(h2[c, 0], weights, preferred_element_type=F32)
 
@@ -278,6 +277,12 @@
                 rec[i] = jnp.dot(past[i], matrix, precision=HIGHEST, preferred_element_type=F32)
             recent = rec[0] if w == 1 else rec[0] + rec[1]
 
+        real, imag = inv_ref[w, 0], inv_ref[w, 1]
+        advance = jnp.concatenate(
+            [jnp.concatenate([real, -imag], axis=1), jnp.concatenate([imag, real], axis=1)], axis=0
+        )
+        coarse = advance.astype(BF16)
+        advance = jnp.concatenate([coarse, (advance - coarse.astype(F32)).astype(BF16), coarse], axis=1)
         totals = [None, None]
         for c, (first, last) in enumerate(cuts):
             for m in range(2):
@@ -316,12 +321,13 @@
 
         current = jnp.concatenate([local[b][m] for m in range(2) for b in range(own)], axis=0)
         moved = current + STEP_WIDTH * total
-        real, imag = inv_ref[w, 0], inv_ref[w, 1]
-        advance = jnp.concatenate(
-            [jnp.concatenate([real, -imag], axis=1), jnp.concatenate([imag, real], axis=1)], axis=0
-        )
+        high = moved.astype(BF16)
+        low = (moved - high.astype(F32)).astype(BF16)
         new = lax.dot_general(
-            moved, advance, (((1,), (1,)), ((), ())), precision=HIGHEST, preferred_element_type=F32
+            jnp.concatenate([high, high, low], axis=1),
+            advance,
+            (((1,), (1,)), ((), ())),
+            preferred_element_type=F32,
         )
         past.append(new)
         split = new.reshape(2, own, slab, pair)

time: 80.1 us -> 78.3 us (0.978)
  Pallas kernels: 76.5 us -> 75.2 us
    pallas_call x1, Pallas kernels: 76.5 us -> 75.2 us  [body(): pl.pallas_call(functools.partial(kernel, dims), out_shape=jax.ShapeDtypeS...]
where the time goes in v6:
time: 78.3 us; the launch traced here: 77.2 us
  Pallas kernels  75.2 us (96%)
  local copies, waits for them, and re-layouts  1.38 us (2%)
    pallas_call x1, Pallas kernels, body(): pl.pallas_call(functools.partial(kernel, dims), out_shape=jax.ShapeDtypeS...  75.2 us

profile of v6, /device:TPU:1, one launch (start us, length us, event | category | flops | bytes accessed | tf_op | source)
XLA Modules:
  0.0 77.2 jit_solution(1933063792996131596)
XLA Ops:
  0.7 75.2 %shard_map.64 = f32[2,16,256]{2,1,0:T(8,128)} custom-call(bf16[8192,128]{1,0:T(8,128)(2,1)} %bitcast.1, f32[2,16,256]{2,1,0:T(8,128)} %row_hbm.1, f32[2,64]{1,0:T(2,128)} %coup_hbm.1, f32[3,2,64,64]{3,2,1,0:T(8,128)} %inv_hbm.1, s32[1]{0:T(128)S(6)} %copy.8.start_hbm, s32[4]{0:T(128)} %time_hbm.1), custom_call_target="tpu_custom_call" | custom-call | tf_op jit(solution)/shard_map/pallas_call | solution.py:366
  75.8 1.4 %copy.9 = f32[2,16,256]{2,1,0:T(8,128)} copy(f32[2,16,256]{2,1,0:T(8,128)} %shard_map.64) | data formatting | bytes 65536

commit v7 on v6

--- a/solution.py
+++ b/solution.py
@@ -85,13 +85,11 @@
     z = h // n_y
     y = lax.rem(h, n_y)
 
-    def outward(k, n):
-        step = (k + 1) // 2
-        return n // 2 + step - 2 * step * lax.rem(k, 2)
-
-    def second_peer(k):
-        x = lax.rem(sec // 2 + outward(k // 2, n_second // 2), n_second // 2)
-        return x * 2 + lax.rem(lax.rem(sec, 2) + 1 - lax.rem(k, 2), 2)
+    n_x = n_second // 2
+    across = sorted(((dx, dc) for dx in range(n_x) for dc in range(2) if dx or dc), key=lambda d: -min(d[0], n_x - d[0]))
+
+    def second_peer(d):
+        return lax.rem(sec // 2 + d[0], n_x) * 2 + lax.rem(lax.rem(sec, 2) + d[1], 2)
 
     far_first = sorted(((dz, dy) for dz in range(n_z) for dy in range(n_y) if dz or dy), key=lambda d: -min(d[0], n_z - d[0]) - min(d[1], n_y - d[1]))
 
@@ -101,9 +99,8 @@
         to = lax.rem(z + dz, n_z) * n_y + lax.rem(y + dy, n_y)
         pl.semaphore_signal(barrier, 1, device_id=(to, sec), device_id_type=MESH)
 
-    @pl.loop(0, n_second - 1)
-    def _(k):
-        pl.semaphore_signal(barrier, 1, device_id=(h, second_peer(k)), device_id_type=MESH)
+    for d in across:
+        pl.semaphore_signal(barrier, 1, device_id=(h, second_peer(d)), device_id_type=MESH)
 
     loads = [
         pltpu.make_async_copy(src, dst, in_sem.at[i])
@@ -146,10 +143,9 @@
     def send_energy(w):
         mine = ebuf.at[w, pl.ds(pl.multiple_of(sec * slab, slab), slab)]
 
-        @pl.loop(0, n_second - 1)
-        def _(k):
+        for d in across:
             pltpu.make_async_remote_copy(
-                mine, mine, a_send.at[w], a_recv.at[w], device_id=(h, second_peer(k)), device_id_type=MESH
+                mine, mine, a_send.at[w], a_recv.at[w], device_id=(h, second_peer(d)), device_id_type=MESH
             ).start()
 
     part = 2 * slab * (n_z // len(cuts)) * own

time: 78.3 us -> 79.8 us (1.019); the launches traced: 77.2 us -> 79.7 us
  Pallas kernels: 75.2 us -> 77.6 us
    pallas_call x1, Pallas kernels: 75.2 us -> 77.6 us  [body(): pl.pallas_call(functools.partial(kernel, dims), out_shape=jax.ShapeDtypeS...]
where the time goes in v7:
time: 79.8 us; the launch traced here: 79.7 us
  Pallas kernels  77.6 us (97%)
  local copies, waits for them, and re-layouts  1.38 us (2%)
    pallas_call x1, Pallas kernels, body(): pl.pallas_call(functools.partial(kernel, dims), out_shape=jax.ShapeDtypeS...  77.6 us

profile of v7, /device:TPU:1, one launch (start us, length us, event | category | flops | bytes accessed | tf_op | source)
XLA Modules:
  0.0 79.7 jit_solution(2932070012448410133)
XLA Ops:
  0.7 77.6 %shard_map.64 = f32[2,16,256]{2,1,0:T(8,128)} custom-call(bf16[8192,128]{1,0:T(8,128)(2,1)} %bitcast.1, f32[2,16,256]{2,1,0:T(8,128)} %row_hbm.1, f32[2,64]{1,0:T(2,128)} %coup_hbm.1, f32[3,2,64,64]{3,2,1,0:T(8,128)} %inv_hbm.1, s32[1]{0:T(128)S(6)} %copy.8.start_hbm, s32[4]{0:T(128)} %time_hbm.1), custom_call_target="tpu_custom_call" | custom-call | tf_op jit(solution)/shard_map/pallas_call | solution.py:362
  78.3 1.4 %copy.9 = f32[2,16,256]{2,1,0:T(8,128)} copy(f32[2,16,256]{2,1,0:T(8,128)} %shard_map.64) | data formatting | bytes 65536
